TPU v7x, 256 devices: a whole 4x4x8 slice. The times are simulated.
256 devices in a mesh: txt: 8 (over z), clip: 8 (over x, core), proj: 4 (over y).
Axes of the slice: x: 4, y: 4, z: 8, core: 2. Of those that a mesh axis runs over, the one named last changes fastest.
Arguments:
- text_hidden: float32 [8192, 1024], P(('txt', 'clip')), may hold values from -16 to 16
- proj_weight: float32 [1024, 1024], P(None, 'proj'), may hold values from -2 to 2
- clip_embed: float32 [8192, 1024], P(('txt', 'clip'), 'proj'), may hold values from -16 to 16
- positive: int32 [8192], P(('txt', 'clip')), may hold values from 0 to 8191, each once
- logit_scale: float32 [1], replicated, may hold values from 10 to 300
Outputs:
- grad_hidden: float32 [8192, 1024], P(('txt', 'clip'), 'proj')
- grad_weight: float32 [1024, 1024], P(('txt', 'clip'), 'proj')
- grad_clip: float32 [8192, 1024], P(('txt', 'clip'), 'proj')
Inputs may be any that keep to these rules, and one draw needn't show every extreme that they name: `positive`: each clip row is the match of exactly one text row.
All inputs are finite; a program needn't handle non-finite values.
Results may differ from a plain program's by a relative error of at most 0.0003.
Values sent between devices are 32-bit elements; how exact they have to be, the bound alone decides.
A program may use at most 64 MiB of HBM per device.

v0:
```python
import jax
import jax.numpy as jnp
from jax import lax
from jax.sharding import PartitionSpec as P

EPSILON = 1e-06
PRECISE = lax.Precision.HIGHEST


def in_order(blocks, dim):
    lengths = list(blocks.shape[1:])
    lengths[dim] *= blocks.shape[0]
    return jnp.moveaxis(blocks, 0, dim).reshape(lengths)


def sent_to_all(array, axis):
    size = lax.axis_size(axis)
    return lax.all_to_all(
        jnp.broadcast_to(array[None], (size, *array.shape)), axis, 0, 0, tiled=True
    )


def gather_directly(array, axis, dim):
    return in_order(sent_to_all(array, axis), dim)


def all_in_one(array, axis):
    leaves = jax.tree.leaves(array)
    order = sorted(range(len(leaves)), key=lambda k: -leaves[k].size)
    width = (1, *leaves[order[0]].shape)[-1]
    lines = [
        jnp.pad(leaves[k].reshape(-1), (0, -leaves[k].size % width)).reshape(-1, width)
        for k in order
    ]
    both, at, found = (sent_to_all(jnp.concatenate(lines), axis), 0, {})
    for k, line in zip(order, lines):
        section = both[:, at : at + len(line)].reshape(len(both), -1)
        found[k] = section[:, : leaves[k].size].reshape(-1, *leaves[k].shape)
        at += len(line)
    numbers = iter(range(len(leaves)))
    return jax.tree.map(lambda _: found[next(numbers)], array)


def combined_pairwise(pieces, combine):
    while len(jax.tree.leaves(pieces)[0]) > 1:
        pieces = jax.vmap(combine)(
            *(jax.tree.map(lambda part: part[side::2], pieces) for side in (0, 1))
        )
    return jax.tree.map(lambda part: part[0], pieces)


def combined_all(array, axis, combine):
    pieces = all_in_one(array, axis)
    return combined_pairwise(pieces, combine)


def cut_along(array, dim, size):
    lengths = array.shape
    blocks = array.reshape(*lengths[:dim], size, lengths[dim] // size, *lengths[dim + 1 :])
    return jnp.moveaxis(blocks, dim, 0)


def sent_and_summed(array, axis, dim):
    size = lax.axis_size(axis)
    blocks = lax.all_to_all(cut_along(array, dim, size), axis, 0, 0, tiled=True)
    return jnp.sum(blocks, axis=0)


def unit_rows(raw):
    inverse = lax.rsqrt(jnp.sum(raw * raw, axis=1, keepdims=True) + EPSILON)
    return (raw * inverse, inverse)


def unit_back(unit, inverse, upstream):
    along = jnp.sum(unit * upstream, axis=1, keepdims=True)
    return (upstream - unit * along) * inverse


def paired_stats(earlier, later):
    top = jnp.maximum(earlier[0], later[0])
    total = earlier[1] * jnp.exp(earlier[0] - top) + later[1] * jnp.exp(later[0] - top)
    return (top, total)


def body(text_hidden, proj_weight, clip_embed, positive, logit_scale):
    score_scale = logit_scale[0]
    clip_groups = lax.axis_size("clip")
    proj_groups = lax.axis_size("proj")
    sub_rows = text_hidden.shape[0]
    quarter = sub_rows // proj_groups
    projected = jnp.dot(
        text_hidden, proj_weight, precision=PRECISE, preferred_element_type=jnp.float32
    )
    text_rows, clip_rows = (
        lax.all_to_all(projected, "proj", split_axis=0, concat_axis=1, tiled=True),
        lax.all_to_all(clip_embed, "proj", split_axis=0, concat_axis=1, tiled=True),
    )
    text_unit, text_inverse = unit_rows(text_rows)
    clip_unit, clip_inverse = unit_rows(clip_rows)
    own_proj = lax.axis_index("proj")
    own_clip = lax.axis_index("clip")
    own_positive = lax.dynamic_slice_in_dim(positive, own_proj * quarter, quarter)
    clip_near = gather_directly(clip_unit, "txt", 0)
    text_tile, positive_tile = (
        lax.all_gather(text_unit, ("clip", "proj"), axis=0, tiled=True),
        lax.all_gather(own_positive, ("clip", "proj"), axis=0, tiled=True),
    )
    block_index = positive_tile // sub_rows
    remainder = positive_tile % sub_rows
    inside = (block_index % clip_groups == own_clip) & (remainder // quarter == own_proj)
    column = jnp.where(inside, block_index // clip_groups * quarter + remainder % quarter, -1)
    scores = score_scale * lax.dot_general(
        text_tile,
        clip_near,
        (((1,), (1,)), ((), ())),
        precision=PRECISE,
        preferred_element_type=jnp.float32,
    )
    local_row_max = jnp.max(scores, axis=1)
    local_col_max = jnp.max(scores, axis=0)
    row_local = (local_row_max, jnp.sum(jnp.exp(scores - local_row_max[:, None]), axis=1))
    row_max, row_total = combined_all(row_local, ("clip", "proj"), paired_stats)
    col_local = (local_col_max, jnp.sum(jnp.exp(scores - local_col_max[None, :]), axis=0))
    col_max, col_total = combined_all(col_local, "txt", paired_stats)
    row_exp = jnp.exp(scores - row_max[:, None])
    col_exp = jnp.exp(scores - col_max[None, :])
    matches = (lax.broadcasted_iota(jnp.int32, scores.shape, 1) == column[:, None]).astype(
        jnp.float32
    )
    grad_scores = 0.5 * (row_exp / row_total[:, None] + col_exp / col_total[None, :]) - matches
    text_cot = lax.psum_scatter(
        score_scale
        * jnp.dot(grad_scores, clip_near, precision=PRECISE, preferred_element_type=jnp.float32),
        ("clip", "proj"),
        scatter_dimension=0,
        tiled=True,
    )
    clip_cot = sent_and_summed(
        score_scale
        * lax.dot_general(
            grad_scores,
            text_tile,
            (((0,), (0,)), ((), ())),
            precision=PRECISE,
            preferred_element_type=jnp.float32,
        ),
        "txt",
        0,
    )
    text_back = unit_back(text_unit, text_inverse, text_cot)
    clip_back = unit_back(clip_unit, clip_inverse, clip_cot)
    text_cols, grad_clip = (
        lax.all_to_all(text_back, "proj", split_axis=1, concat_axis=0, tiled=True),
        lax.all_to_all(clip_back, "proj", split_axis=1, concat_axis=0, tiled=True),
    )
    grad_weight = sent_and_summed(
        lax.dot_general(
            text_hidden,
            text_cols,
            (((0,), (0,)), ((), ())),
            precision=PRECISE,
            preferred_element_type=jnp.float32,
        ),
        ("txt", "clip"),
        0,
    )
    partial_hidden = lax.dot_general(
        text_cols,
        proj_weight,
        (((1,), (1,)), ((), ())),
        precision=PRECISE,
        preferred_element_type=jnp.float32,
    )
    grad_hidden = sent_and_summed(partial_hidden, "proj", 1)
    return (grad_hidden, grad_weight, grad_clip)


def solution(mesh):
    in_specs = (
        P(("txt", "clip"), None),
        P(None, "proj"),
        P(("txt", "clip"), "proj"),
        P(("txt", "clip")),
        P(),
    )
    out_specs = (P(("txt", "clip"), "proj"), P(("txt", "clip"), "proj"), P(("txt", "clip"), "proj"))
    return jax.shard_map(body, mesh=mesh, in_specs=in_specs, out_specs=out_specs, check_vma=False)
```

profile of v0, /device:TPU:1, one launch (start us, length us, event | category | flops | bytes accessed | tf_op | source)
XLA Modules:
  0.0 288.7 jit_solution(14806833728530572804)
XLA Ops:
  10.1 9.6 %all_to_all.103 = f32[4,32,256]{2,1,0:T(8,128)S(1)} all-to-all(f32[4,32,256]{2,1,0:T(8,128)S(1)} %bitcast.94), channel_id=1, replica_groups=mesh['txt'=8,'clip'=8,'proj'=4] {'proj'}, dimensions={0} | all-to-all | bytes 262144 | tf_op jit(solution)/shard_map/all_to_all | solution.py:95
  20.6 8.1 %all_to_all.104 = f32[4,32,256]{2,1,0:T(8,128)S(1)} all-to-all(f32[4,32,256]{2,1,0:T(8,128)} %bitcast.95), channel_id=1, replica_groups=mesh['txt'=8,'clip'=8,'proj'=4] {'proj'}, dimensions={0} | all-to-all | bytes 262144 | tf_op jit(solution)/shard_map/all_to_all | solution.py:96
  30.1 8.2 %all-to-all-start.2 = ((f32[8,32,1024]{2,1,0:T(8,128)}), f32[8,32,1024]{2,1,0:T(8,128)S(1)}, u32[]{:S(2)}, u32[]{:S(2)}) async-start(f32[8,32,1024]{2,1,0:T(8,128)} %broadcast_in_dim.8), calls=%async_computation.2 | async-start | bytes 2097152 | tf_op jit(solution)/shard_map/all_to_all | solution.py:18
  40.4 17.2 %all-reduce = s32[1024]{0:T(1024)S(1)} all-reduce(s32[1024]{0:T(1024)S(1)} %dynamic-slice_dynamic-update-slice_fusion), channel_id=1, replica_groups=mesh['txt'=8,'clip'=8,'proj'=4] {'clip','proj'}, use_global_device_ids=true, to_apply=%add | all-reduce | flops 1024 | bytes 8192
  57.6 6.9 %all-to-all-done.2 = f32[8,32,1024]{2,1,0:T(8,128)S(1)} async-done(((f32[8,32,1024]{2,1,0:T(8,128)}), f32[8,32,1024]{2,1,0:T(8,128)S(1)}, u32[]{:S(2)}, u32[]{:S(2)}) %all-to-all-start.2) | async-done | bytes 1048608 | tf_op jit(solution)/shard_map/all_to_all | solution.py:18
  64.4 10.2 %all-gather.2.cloned.1.call-done = f32[1024,1024]{1,0:T(8,128)} async-done(((f32[32,1024]{1,0:T(8,128)}), f32[1024,1024]{1,0:T(8,128)}) %all-gather.2.cloned.1.call-update) | async-done | bytes 4194320 | tf_op jit(solution)/shard_map/all_gather | solution.py:105
  74.7 5.4 %fusion.16 = (f32[1024]{0:T(1024)S(1)}, f32[256]{0:T(256)S(1)}, f32[1024,256]{1,0:T(8,128)S(1)}) fusion(f32[1024,1024]{1,0:T(8,128)} %all-gather.2.cloned.1.call-done, f32[256,1024]{1,0:T(8,128)S(1)} %bitcast.79, f32[]{:T(128)} %bitcast.76), kind=kOutput, calls=%fused_computation.74 | convolution fusion | flops 3222010624 | bytes 6296580 | tf_op jit(solution)/shard_map/dot_general | solution.py:112
  81.2 6.7 %all-to-all-start.4 = ((f32[8,2,256]{2,1,0:T(2,128)}), f32[8,2,256]{2,1,0:T(2,128)S(1)}, u32[]{:S(2)}, u32[]{:S(2)}) async-start(f32[8,2,256]{2,1,0:T(2,128)} %broadcast_in_dim.10), calls=%async_computation.4 | async-start | bytes 32768 | tf_op jit(solution)/shard_map/all_to_all | solution.py:18
  87.9 6.6 %all-to-all-done.4 = f32[8,2,256]{2,1,0:T(2,128)S(1)} async-done(((f32[8,2,256]{2,1,0:T(2,128)}), f32[8,2,256]{2,1,0:T(2,128)S(1)}, u32[]{:S(2)}, u32[]{:S(2)}) %all-to-all-start.4) | async-done | bytes 16416 | tf_op jit(solution)/shard_map/all_to_all | solution.py:18
  95.3 6.7 %all-to-all-start.3 = ((f32[32,2,1024]{2,1,0:T(2,128)}), f32[32,2,1024]{2,1,0:T(2,128)}, u32[]{:S(2)}, u32[]{:S(2)}) async-start(f32[32,2,1024]{2,1,0:T(2,128)} %broadcast_in_dim.9), calls=%async_computation.3 | async-start | bytes 524288 | tf_op jit(solution)/shard_map/all_to_all | solution.py:18
  103.1 7.8 %all-to-all-done.3 = f32[32,2,1024]{2,1,0:T(2,128)} async-done(((f32[32,2,1024]{2,1,0:T(2,128)}), f32[32,2,1024]{2,1,0:T(2,128)}, u32[]{:S(2)}, u32[]{:S(2)}) %all-to-all-start.3) | async-done | bytes 262176 | tf_op jit(solution)/shard_map/all_to_all | solution.py:18
  120.6 6.3 %convolution_multiply_fusion = f32[1024,1024]{1,0:T(8,128)} fusion(f32[256,1024]{1,0:T(8,128)S(1)} %bitcast.80, f32[]{:T(128)} %bitcast.75, f32[1024,256]{1,0:T(8,128)S(1)} %get-tuple-element.27, s32[1024]{0:T(1024)S(1)} %fusion.8, f32[256]{0:T(256)S(1)} %bitcast.104, f32[256]{0:T(256)} %bitcast.106, f32[1024]{0:T(1024)S(1)} %bitcast.99, f32[1024]{0:T(1024)S(1)} %bitcast.101), kind=kOutput, calls=%fused_computation | convolution fusion | flops 3224633344 | bytes 6305796 | tf_op jit(solution)/shard_map/dot_general | solution.py:133
  127.5 6.3 %convolution_multiply_fusion.1 = f32[256,1024]{1,0:T(8,128)S(1)} fusion(f32[1024,1024]{1,0:T(8,128)} %all-gather.2.cloned.1.call-done, f32[]{:T(128)} %bitcast.77, f32[1024,256]{1,0:T(8,128)S(1)} %get-tuple-element.27, s32[1024]{0:T(1024)S(1)} %fusion.8, f32[256]{0:T(256)S(1)} %bitcast.105, f32[256]{0:T(256)S(1)} %bitcast.107, f32[1024]{0:T(1024)S(1)} %bitcast.100, ...), kind=kOutput, calls=%fused_computation.1 | convolution fusion | flops 3223846912 | bytes 6305796 | tf_op jit(solution)/shard_map/dot_general | solution.py:140
  133.9 31.1 %all_to_all.105 = f32[8,32,1024]{2,1,0:T(8,128)S(1)} all-to-all(f32[8,32,1024]{2,1,0:T(8,128)S(1)} %bitcast.90), channel_id=1, replica_groups=mesh['txt'=8,'clip'=8,'proj'=4] {'txt'}, dimensions={0} | all-to-all | bytes 2097152 | tf_op jit(solution)/shard_map/all_to_all | solution.py:65
  165.3 42.5 %reduce-scatter.2.cloned.1.call-done = f32[32,1024]{1,0:T(8,128)} async-done(((f32[1024,1024]{1,0:T(8,128)}), f32[32,1024]{1,0:T(8,128)}) %reduce-scatter.2.cloned.1.call-update) | async-done | bytes 131088 | tf_op jit(solution)/shard_map/reduce_scatter | solution.py:131
  210.5 3.3 %all-to-all-start.5 = ((f32[32,4,256]{2,0,1:T(8,128)}), f32[32,4,256]{2,0,1:T(8,128)S(1)}, u32[]{:S(2)}, u32[]{:S(2)}) async-start(f32[32,4,256]{2,0,1:T(8,128)} %bitcast.74), calls=%async_computation.6 | async-start | bytes 262144 | tf_op jit(solution)/shard_map/all_to_all | solution.py:153
  214.6 4.0 %all-to-all-done.5 = f32[32,4,256]{2,0,1:T(8,128)S(1)} async-done(((f32[32,4,256]{2,0,1:T(8,128)}), f32[32,4,256]{2,0,1:T(8,128)S(1)}, u32[]{:S(2)}, u32[]{:S(2)}) %all-to-all-start.5) | async-done | bytes 131104 | tf_op jit(solution)/shard_map/all_to_all | solution.py:153
  218.6 3.3 %all-to-all-start.9 = ((f32[32,4,256]{2,0,1:T(8,128)}), f32[32,4,256]{2,0,1:T(8,128)S(1)}, u32[]{:S(2)}, u32[]{:S(2)}) async-start(f32[32,4,256]{2,0,1:T(8,128)} %fusion), calls=%async_computation.10 | async-start | bytes 262144 | tf_op jit(solution)/shard_map/all_to_all | solution.py:154
  222.0 2.0 convolution_bitcast_fusion.1
  224.0 2.8 all-to-all-done.9
  226.8 3.5 %all-to-all-start.6 = ((f32[4,128,256]{2,1,0:T(8,128)}), f32[4,128,256]{2,1,0:T(8,128)S(1)}, u32[]{:S(2)}, u32[]{:S(2)}) async-start(f32[4,128,256]{2,1,0:T(8,128)} %convolution_bitcast_fusion.1), calls=%async_computation.7 | async-start | bytes 1048576 | tf_op jit(solution)/shard_map/all_to_all | solution.py:65
  232.6 4.5 %all-to-all-done.6 = f32[4,128,256]{2,1,0:T(8,128)S(1)} async-done(((f32[4,128,256]{2,1,0:T(8,128)}), f32[4,128,256]{2,1,0:T(8,128)S(1)}, u32[]{:S(2)}, u32[]{:S(2)}) %all-to-all-start.6) | async-done | bytes 524320 | tf_op jit(solution)/shard_map/all_to_all | solution.py:65
  237.1 15.4 %all-to-all-start.7 = ((f32[64,16,256]{2,1,0:T(8,128)}), f32[64,16,256]{2,1,0:T(8,128)S(1)}, u32[]{:S(2)}, u32[]{:S(2)}) async-start(f32[64,16,256]{2,1,0:T(8,128)} %bitcast.24), calls=%async_computation.8 | async-start | bytes 2097152 | tf_op jit(solution)/shard_map/all_to_all | solution.py:65
  253.2 27.3 %all-to-all-done.7 = f32[64,16,256]{2,1,0:T(8,128)S(1)} async-done(((f32[64,16,256]{2,1,0:T(8,128)}), f32[64,16,256]{2,1,0:T(8,128)S(1)}, u32[]{:S(2)}, u32[]{:S(2)}) %all-to-all-start.7) | async-done | bytes 1048608 | tf_op jit(solution)/shard_map/all_to_all | solution.py:65
  (80 shorter events, 27.2 us)
Async XLA Ops:
  7.2 1.2 copy-start
  7.2 31.7 %copy-start.4 = (u32[256]{0:T(256)S(1)}, u32[256]{0:T(256)}, u32[]{:S(2)}) copy-start(u32[256]{0:T(256)} %constant.89) | copy-start | bytes 3076
  7.2 33.0 %copy-start.3 = (s32[128]{0:T(128)S(1)}, s32[128]{0:T(128)}, u32[]{:S(2)}) copy-start(s32[128]{0:T(128)} %param.8) | copy-start | bytes 1540
  7.2 67.5 %all-gather.2.cloned.1.call-start = ((), (), s32[]{:S(2)}) async-start(), calls=%async_computation.11 | async-start | bytes 4325376 | tf_op jit(solution)/shard_map/all_gather | solution.py:105
  30.1 34.3 %all-to-all-start.2 = ((f32[8,32,1024]{2,1,0:T(8,128)}), f32[8,32,1024]{2,1,0:T(8,128)S(1)}, u32[]{:S(2)}, u32[]{:S(2)}) async-start(f32[8,32,1024]{2,1,0:T(8,128)} %broadcast_in_dim.8), calls=%async_computation.2 | async-start | bytes 2097152 | tf_op jit(solution)/shard_map/all_to_all | solution.py:18
  81.2 13.4 %all-to-all-start.4 = ((f32[8,2,256]{2,1,0:T(2,128)}), f32[8,2,256]{2,1,0:T(2,128)S(1)}, u32[]{:S(2)}, u32[]{:S(2)}) async-start(f32[8,2,256]{2,1,0:T(2,128)} %broadcast_in_dim.10), calls=%async_computation.4 | async-start | bytes 32768 | tf_op jit(solution)/shard_map/all_to_all | solution.py:18
  95.3 15.6 %all-to-all-start.3 = ((f32[32,2,1024]{2,1,0:T(2,128)}), f32[32,2,1024]{2,1,0:T(2,128)}, u32[]{:S(2)}, u32[]{:S(2)}) async-start(f32[32,2,1024]{2,1,0:T(2,128)} %broadcast_in_dim.9), calls=%async_computation.3 | async-start | bytes 524288 | tf_op jit(solution)/shard_map/all_to_all | solution.py:18
  102.0 105.7 %reduce-scatter.2.cloned.1.call-start = ((), (), s32[]{:S(2)}) async-start(), calls=%async_computation.12 | async-start | bytes 4325376 | tf_op jit(solution)/shard_map/reduce_scatter | solution.py:131
  126.8 0.7 copy-start.2
  133.9 96.4 %copy-start.1 = (f32[128,1024]{1,0:T(8,128)S(1)}, f32[128,1024]{1,0:T(8,128)}, u32[]{:S(2)}) copy-start(f32[128,1024]{1,0:T(8,128)} %param.5) | copy-start | bytes 1572868
  210.5 8.1 %all-to-all-start.5 = ((f32[32,4,256]{2,0,1:T(8,128)}), f32[32,4,256]{2,0,1:T(8,128)S(1)}, u32[]{:S(2)}, u32[]{:S(2)}) async-start(f32[32,4,256]{2,0,1:T(8,128)} %bitcast.74), calls=%async_computation.6 | async-start | bytes 262144 | tf_op jit(solution)/shard_map/all_to_all | solution.py:153
  218.6 8.1 %all-to-all-start.9 = ((f32[32,4,256]{2,0,1:T(8,128)}), f32[32,4,256]{2,0,1:T(8,128)S(1)}, u32[]{:S(2)}, u32[]{:S(2)}) async-start(f32[32,4,256]{2,0,1:T(8,128)} %fusion), calls=%async_computation.10 | async-start | bytes 262144 | tf_op jit(solution)/shard_map/all_to_all | solution.py:154
  226.8 10.4 %all-to-all-start.6 = ((f32[4,128,256]{2,1,0:T(8,128)}), f32[4,128,256]{2,1,0:T(8,128)S(1)}, u32[]{:S(2)}, u32[]{:S(2)}) async-start(f32[4,128,256]{2,1,0:T(8,128)} %convolution_bitcast_fusion.1), calls=%async_computation.7 | async-start | bytes 1048576 | tf_op jit(solution)/shard_map/all_to_all | solution.py:65
  237.1 43.4 %all-to-all-start.7 = ((f32[64,16,256]{2,1,0:T(8,128)}), f32[64,16,256]{2,1,0:T(8,128)S(1)}, u32[]{:S(2)}, u32[]{:S(2)}) async-start(f32[64,16,256]{2,1,0:T(8,128)} %bitcast.24), calls=%async_computation.8 | async-start | bytes 2097152 | tf_op jit(solution)/shard_map/all_to_all | solution.py:65
Sparse Core Ops, SparseCore 0:
  20.8 53.8 all-gather.1
  127.0 80.7 reduce-scatter.1
where the time goes:
time: 290 us; the launch traced here: 289 us
  waiting for transfers between devices  113 us (39%)
  blocking collectives  66.1 us (23%)
  starting transfers between devices  47.4 us (16%)
  matrix products  22.7 us (8%)
  local copies, waits for them, and re-layouts  15.8 us (5%)
  between operations  15.6 us (5%)
  other arithmetic  8.45 us (3%)
    reduce_scatter x1, waiting for transfers between devices, body(): lax.psum_scatter(score_scale * jnp.dot(grad_scores, clip_near, precision=...  42.5 us
    all_to_all x2, waiting for transfers between devices, sent_and_summed(): blocks = lax.all_to_all(cut_along(array, dim, size), axis, 0, 0, tiled=True)  31.8 us
    all_to_all x1, blocking collectives, sent_and_summed(): blocks = lax.all_to_all(cut_along(array, dim, size), axis, 0, 0, tiled=True)  31.1 us
    all_to_all x3, starting transfers between devices, sent_to_all(): lax.all_to_all(jnp.broadcast_to(array[None], (size, *array.shape)), axis,...  21.7 us
    all_to_all x3, waiting for transfers between devices, sent_to_all(): lax.all_to_all(jnp.broadcast_to(array[None], (size, *array.shape)), axis,...  21.3 us
    all_to_all x2, starting transfers between devices, sent_and_summed(): blocks = lax.all_to_all(cut_along(array, dim, size), axis, 0, 0, tiled=True)  18.8 us
    unnamed x1, blocking collectives  17.2 us
    all_gather x1, waiting for transfers between devices, body(): lax.all_gather(text_unit, ('clip', 'proj'), axis=0, tiled=True)  10.2 us
  transfers between devices with their start and end apart: 9, of which 9 were waited for; matrix products, arithmetic and copies ran while one was open for 5% of the time, Pallas kernels for 0%

commit v1 on v0

--- a/solution.py
+++ b/solution.py
@@ -102,7 +102,12 @@
     own_positive = lax.dynamic_slice_in_dim(positive, own_proj * quarter, quarter)
     clip_near = gather_directly(clip_unit, "txt", 0)
     text_tile, positive_tile = (
-        lax.all_gather(text_unit, ("clip", "proj"), axis=0, tiled=True),
+        jnp.concatenate(
+            lax.all_to_all(
+                jnp.stack([text_unit] * lax.axis_size(("clip", "proj"))), ("clip", "proj"), 0, 0
+            ),
+            axis=0,
+        ),
         lax.all_gather(own_positive, ("clip", "proj"), axis=0, tiled=True),
     )
     block_index = positive_tile // sub_rows

time: 290 us -> 343 us (1.18)
  blocking collectives: 66.1 us -> 88.4 us
  waiting for transfers between devices: 113 us -> 129 us
  starting transfers between devices: 47.4 us -> 61 us
    unnamed x1, blocking collectives: 17.2 us -> 57.2 us
    all_to_all x3, waiting for transfers between devices: 21.3 us -> 40.3 us  [sent_to_all(): lax.all_to_all(jnp.broadcast_to(array[None], (size, *array.shape)), axis,...]
    all_to_all x2 -> x0, blocking collectives: 17.8 us -> none  [the longest x1 9.64 us: body(): lax.all_to_all(projected, 'proj', split_axis=0, concat_axis=1, tiled=True)]
    all_to_all x0 -> x3, starting transfers between devices: none -> 17.3 us  [the longest x1 8.82 us: body(): lax.all_to_all(jnp.stack([text_unit] * lax.axis_size(('clip', 'proj'))),...]
    all_gather x1 -> x0, waiting for transfers between devices: 10.2 us -> none  [body(): lax.all_gather(text_unit, ('clip', 'proj'), axis=0, tiled=True)]
    all_to_all x0 -> x3, waiting for transfers between devices: none -> 7.05 us  [the longest x1 4.56 us: body(): lax.all_to_all(projected, 'proj', split_axis=0, concat_axis=1, tiled=True)]
    all_to_all x3, starting transfers between devices: 21.7 us -> 17.9 us  [sent_to_all(): lax.all_to_all(jnp.broadcast_to(array[None], (size, *array.shape)), axis,...]
  transfers between devices with their start and end apart: 9 -> 11, of which waited for: 9 -> 10; matrix products, arithmetic and copies ran while one was open for 5% -> 5% of each run, Pallas kernels for 0% -> 0%
where the time goes in v1:
time: 343 us; the launch traced here: 342 us
  waiting for transfers between devices  129 us (38%)
  blocking collectives  88.4 us (26%)
  starting transfers between devices  61 us (18%)
  matrix products  23.4 us (7%)
  local copies, waits for them, and re-layouts  17.1 us (5%)
  between operations  15.6 us (5%)
  other arithmetic  7.79 us (2%)
    unnamed x1, blocking collectives  57.2 us
    reduce_scatter x1, waiting for transfers between devices, body(): lax.psum_scatter(score_scale * jnp.dot(grad_scores, clip_near, precision=...  42.5 us
    all_to_all x3, waiting for transfers between devices, sent_to_all(): lax.all_to_all(jnp.broadcast_to(array[None], (size, *array.shape)), axis,...  40.3 us
    all_to_all x2, waiting for transfers between devices, sent_and_summed(): blocks = lax.all_to_all(cut_along(array, dim, size), axis, 0, 0, tiled=True)  31.8 us
    all_to_all x1, blocking collectives, sent_and_summed(): blocks = lax.all_to_all(cut_along(array, dim, size), axis, 0, 0, tiled=True)  31.1 us
    all_to_all x2, starting transfers between devices, sent_and_summed(): blocks = lax.all_to_all(cut_along(array, dim, size), axis, 0, 0, tiled=True)  18.8 us
    all_to_all x3, starting transfers between devices, sent_to_all(): lax.all_to_all(jnp.broadcast_to(array[None], (size, *array.shape)), axis,...  17.9 us
    all_to_all x1, starting transfers between devices, body(): lax.all_to_all(jnp.stack([text_unit] * lax.axis_size(('clip', 'proj'))),...  8.82 us
  transfers between devices with their start and end apart: 11, of which 10 were waited for; matrix products, arithmetic and copies ran while one was open for 5% of the time, Pallas kernels for 0%

profile of v1, /device:TPU:1, one launch (start us, length us, event | category | flops | bytes accessed | tf_op | source)
XLA Modules:
  0.0 341.7 jit_solution(7834659856175701893)
XLA Ops:
  7.2 5.2 %all-to-all-start.2 = ((f32[4,32,256]{2,1,0:T(8,128)}), f32[4,32,256]{2,1,0:T(8,128)S(1)}, u32[]{:S(2)}, u32[]{:S(2)}) async-start(f32[4,32,256]{2,1,0:T(8,128)} %bitcast.95), calls=%async_computation.2 | async-start | bytes 262144 | tf_op jit(solution)/shard_map/all_to_all | solution.py:96
  17.2 3.3 all-to-all-start
  20.7 4.6 %all-to-all-done = f32[4,32,256]{2,1,0:T(8,128)S(1)} async-done(((f32[4,32,256]{2,1,0:T(8,128)}), f32[4,32,256]{2,1,0:T(8,128)S(1)}, u32[]{:S(2)}, u32[]{:S(2)}) %all-to-all-start) | async-done | bytes 131104 | tf_op jit(solution)/shard_map/all_to_all | solution.py:95
  26.4 8.2 %all-to-all-start.3 = ((f32[8,32,1024]{2,1,0:T(8,128)}), f32[8,32,1024]{2,1,0:T(8,128)S(1)}, u32[]{:S(2)}, u32[]{:S(2)}) async-start(f32[8,32,1024]{2,1,0:T(8,128)} %broadcast_in_dim.8), calls=%async_computation.3 | async-start | bytes 2097152 | tf_op jit(solution)/shard_map/all_to_all | solution.py:18
  34.8 25.9 %all-to-all-done.3 = f32[8,32,1024]{2,1,0:T(8,128)S(1)} async-done(((f32[8,32,1024]{2,1,0:T(8,128)}), f32[8,32,1024]{2,1,0:T(8,128)S(1)}, u32[]{:S(2)}, u32[]{:S(2)}) %all-to-all-start.3) | async-done | bytes 1048608 | tf_op jit(solution)/shard_map/all_to_all | solution.py:18
  63.2 8.8 %all-to-all-start.1 = ((f32[32,32,1024]{2,1,0:T(8,128)}), f32[32,32,1024]{2,1,0:T(8,128)}, u32[]{:S(2)}, u32[]{:S(2)}) async-start(f32[32,32,1024]{2,1,0:T(8,128)} %stack.2), calls=%async_computation.1 | async-start | bytes 8388608 | tf_op jit(solution)/shard_map/all_to_all | solution.py:106
  74.2 57.2 %all-reduce = s32[1024]{0:T(1024)S(1)} all-reduce(s32[1024]{0:T(1024)S(1)} %dynamic-slice_dynamic-update-slice_fusion), channel_id=1, replica_groups=mesh['txt'=8,'clip'=8,'proj'=4] {'clip','proj'}, use_global_device_ids=true, to_apply=%add | all-reduce | flops 1024 | bytes 8192
  131.4 5.4 %fusion.16 = (f32[1024]{0:T(1024)S(1)}, f32[256]{0:T(256)S(1)}, f32[1024,256]{1,0:T(8,128)S(1)}) fusion(f32[1024,1024]{1,0:T(8,128)} %bitcast.3, f32[256,1024]{1,0:T(8,128)S(1)} %bitcast.80, f32[]{:T(128)} %bitcast.77), kind=kOutput, calls=%fused_computation.74 | convolution fusion | flops 3222010624 | bytes 6296580 | tf_op jit(solution)/shard_map/dot_general | solution.py:117
  137.9 3.3 all-to-all-start.5
  141.3 6.5 %all-to-all-done.5 = f32[8,2,256]{2,1,0:T(2,128)S(1)} async-done(((f32[8,2,256]{2,1,0:T(2,128)}), f32[8,2,256]{2,1,0:T(2,128)S(1)}, u32[]{:S(2)}, u32[]{:S(2)}) %all-to-all-start.5) | async-done | bytes 16416 | tf_op jit(solution)/shard_map/all_to_all | solution.py:18
  148.6 6.4 %all-to-all-start.4 = ((f32[32,2,1024]{2,1,0:T(2,128)}), f32[32,2,1024]{2,1,0:T(2,128)}, u32[]{:S(2)}, u32[]{:S(2)}) async-start(f32[32,2,1024]{2,1,0:T(2,128)} %broadcast_in_dim.9), calls=%async_computation.4 | async-start | bytes 524288 | tf_op jit(solution)/shard_map/all_to_all | solution.py:18
  156.1 7.9 %all-to-all-done.4 = f32[32,2,1024]{2,1,0:T(2,128)} async-done(((f32[32,2,1024]{2,1,0:T(2,128)}), f32[32,2,1024]{2,1,0:T(2,128)}, u32[]{:S(2)}, u32[]{:S(2)}) %all-to-all-start.4) | async-done | bytes 262176 | tf_op jit(solution)/shard_map/all_to_all | solution.py:18
  173.6 6.3 %convolution_multiply_fusion = f32[1024,1024]{1,0:T(8,128)} fusion(f32[256,1024]{1,0:T(8,128)S(1)} %bitcast.81, f32[]{:T(128)} %bitcast.76, f32[1024,256]{1,0:T(8,128)S(1)} %get-tuple-element.27, s32[1024]{0:T(1024)S(1)} %fusion.8, f32[256]{0:T(256)S(1)} %bitcast.104, f32[256]{0:T(256)} %bitcast.106, f32[1024]{0:T(1024)S(1)} %bitcast.99, f32[1024]{0:T(1024)S(1)} %bitcast.101), kind=kOutput, calls=%fused_computation | convolution fusion | flops 3224633344 | bytes 6305796 | tf_op jit(solution)/shard_map/dot_general | solution.py:138
  180.6 6.3 %convolution_multiply_fusion.1 = f32[256,1024]{1,0:T(8,128)S(1)} fusion(f32[1024,1024]{1,0:T(8,128)} %bitcast.3, f32[]{:T(128)} %bitcast.78, f32[1024,256]{1,0:T(8,128)S(1)} %get-tuple-element.27, s32[1024]{0:T(1024)S(1)} %fusion.8, f32[256]{0:T(256)S(1)} %bitcast.105, f32[256]{0:T(256)S(1)} %bitcast.107, f32[1024]{0:T(1024)S(1)} %bitcast.100, ...), kind=kOutput, calls=%fused_computation.1 | convolution fusion | flops 3223846912 | bytes 6305796 | tf_op jit(solution)/shard_map/dot_general | solution.py:145
  186.9 31.1 %all_to_all.108 = f32[8,32,1024]{2,1,0:T(8,128)S(1)} all-to-all(f32[8,32,1024]{2,1,0:T(8,128)S(1)} %bitcast.91), channel_id=1, replica_groups=mesh['txt'=8,'clip'=8,'proj'=4] {'txt'}, dimensions={0} | all-to-all | bytes 2097152 | tf_op jit(solution)/shard_map/all_to_all | solution.py:65
  218.3 42.5 %reduce-scatter.2.cloned.1.call-done = f32[32,1024]{1,0:T(8,128)} async-done(((f32[1024,1024]{1,0:T(8,128)}), f32[32,1024]{1,0:T(8,128)}) %reduce-scatter.2.cloned.1.call-update) | async-done | bytes 131088 | tf_op jit(solution)/shard_map/reduce_scatter | solution.py:136
  263.5 3.3 all-to-all-start.6
  267.6 4.0 %all-to-all-done.6 = f32[32,4,256]{2,0,1:T(8,128)S(1)} async-done(((f32[32,4,256]{2,0,1:T(8,128)}), f32[32,4,256]{2,0,1:T(8,128)S(1)}, u32[]{:S(2)}, u32[]{:S(2)}) %all-to-all-start.6) | async-done | bytes 131104 | tf_op jit(solution)/shard_map/all_to_all | solution.py:158
  271.7 3.3 all-to-all-start.10
  277.0 2.8 all-to-all-done.10
  279.8 3.5 %all-to-all-start.7 = ((f32[4,128,256]{2,1,0:T(8,128)}), f32[4,128,256]{2,1,0:T(8,128)S(1)}, u32[]{:S(2)}, u32[]{:S(2)}) async-start(f32[4,128,256]{2,1,0:T(8,128)} %convolution_bitcast_fusion.1), calls=%async_computation.8 | async-start | bytes 1048576 | tf_op jit(solution)/shard_map/all_to_all | solution.py:65
  285.6 4.5 %all-to-all-done.7 = f32[4,128,256]{2,1,0:T(8,128)S(1)} async-done(((f32[4,128,256]{2,1,0:T(8,128)}), f32[4,128,256]{2,1,0:T(8,128)S(1)}, u32[]{:S(2)}, u32[]{:S(2)}) %all-to-all-start.7) | async-done | bytes 524320 | tf_op jit(solution)/shard_map/all_to_all | solution.py:65
  290.2 15.4 %all-to-all-start.8 = ((f32[64,16,256]{2,1,0:T(8,128)}), f32[64,16,256]{2,1,0:T(8,128)S(1)}, u32[]{:S(2)}, u32[]{:S(2)}) async-start(f32[64,16,256]{2,1,0:T(8,128)} %bitcast.25), calls=%async_computation.9 | async-start | bytes 2097152 | tf_op jit(solution)/shard_map/all_to_all | solution.py:65
  306.2 27.3 %all-to-all-done.8 = f32[64,16,256]{2,1,0:T(8,128)S(1)} async-done(((f32[64,16,256]{2,1,0:T(8,128)}), f32[64,16,256]{2,1,0:T(8,128)S(1)}, u32[]{:S(2)}, u32[]{:S(2)}) %all-to-all-start.8) | async-done | bytes 1048608 | tf_op jit(solution)/shard_map/all_to_all | solution.py:65
  (82 shorter events, 33.0 us)
Async XLA Ops:
  7.2 5.2 %copy-start = (f32[1024,256]{1,0:T(8,128)S(1)}, f32[1024,256]{1,0:T(8,128)}, u32[]{:S(2)}) copy-start(f32[1024,256]{1,0:T(8,128)} %param.6) | copy-start | bytes 3145732
  7.2 10.0 %all-to-all-start.2 = ((f32[4,32,256]{2,1,0:T(8,128)}), f32[4,32,256]{2,1,0:T(8,128)S(1)}, u32[]{:S(2)}, u32[]{:S(2)}) async-start(f32[4,32,256]{2,1,0:T(8,128)} %bitcast.95), calls=%async_computation.2 | async-start | bytes 262144 | tf_op jit(solution)/shard_map/all_to_all | solution.py:96
  17.2 8.1 %all-to-all-start = ((f32[4,32,256]{2,1,0:T(8,128)}), f32[4,32,256]{2,1,0:T(8,128)S(1)}, u32[]{:S(2)}, u32[]{:S(2)}) async-start(f32[4,32,256]{2,1,0:T(8,128)} %bitcast.1), calls=%async_computation | async-start | bytes 262144 | tf_op jit(solution)/shard_map/all_to_all | solution.py:95
  26.4 34.3 %all-to-all-start.3 = ((f32[8,32,1024]{2,1,0:T(8,128)}), f32[8,32,1024]{2,1,0:T(8,128)S(1)}, u32[]{:S(2)}, u32[]{:S(2)}) async-start(f32[8,32,1024]{2,1,0:T(8,128)} %broadcast_in_dim.8), calls=%async_computation.3 | async-start | bytes 2097152 | tf_op jit(solution)/shard_map/all_to_all | solution.py:18
  63.2 9.5 %copy-start.4 = (u32[256]{0:T(256)S(1)}, u32[256]{0:T(256)}, u32[]{:S(2)}) copy-start(u32[256]{0:T(256)} %constant.89) | copy-start | bytes 3076
  63.2 10.7 %copy-start.3 = (s32[128]{0:T(128)S(1)}, s32[128]{0:T(128)}, u32[]{:S(2)}) copy-start(s32[128]{0:T(128)} %param.8) | copy-start | bytes 1540
  63.2 68.2 %all-to-all-start.1 = ((f32[32,32,1024]{2,1,0:T(8,128)}), f32[32,32,1024]{2,1,0:T(8,128)}, u32[]{:S(2)}, u32[]{:S(2)}) async-start(f32[32,32,1024]{2,1,0:T(8,128)} %stack.2), calls=%async_computation.1 | async-start | bytes 8388608 | tf_op jit(solution)/shard_map/all_to_all | solution.py:106
  137.9 9.9 %all-to-all-start.5 = ((f32[8,2,256]{2,1,0:T(2,128)}), f32[8,2,256]{2,1,0:T(2,128)S(1)}, u32[]{:S(2)}, u32[]{:S(2)}) async-start(f32[8,2,256]{2,1,0:T(2,128)} %broadcast_in_dim.10), calls=%async_computation.5 | async-start | bytes 32768 | tf_op jit(solution)/shard_map/all_to_all | solution.py:18
  148.6 15.4 %all-to-all-start.4 = ((f32[32,2,1024]{2,1,0:T(2,128)}), f32[32,2,1024]{2,1,0:T(2,128)}, u32[]{:S(2)}, u32[]{:S(2)}) async-start(f32[32,2,1024]{2,1,0:T(2,128)} %broadcast_in_dim.9), calls=%async_computation.4 | async-start | bytes 524288 | tf_op jit(solution)/shard_map/all_to_all | solution.py:18
  155.0 105.8 %reduce-scatter.2.cloned.1.call-start = ((), (), s32[]{:S(2)}) async-start(), calls=%async_computation.12 | async-start | bytes 4325376 | tf_op jit(solution)/shard_map/reduce_scatter | solution.py:136
  179.9 0.7 copy-start.2
  186.9 96.4 %copy-start.1 = (f32[128,1024]{1,0:T(8,128)S(1)}, f32[128,1024]{1,0:T(8,128)}, u32[]{:S(2)}) copy-start(f32[128,1024]{1,0:T(8,128)} %param.5) | copy-start | bytes 1572868
  263.5 8.1 %all-to-all-start.6 = ((f32[32,4,256]{2,0,1:T(8,128)}), f32[32,4,256]{2,0,1:T(8,128)S(1)}, u32[]{:S(2)}, u32[]{:S(2)}) async-start(f32[32,4,256]{2,0,1:T(8,128)} %bitcast.75), calls=%async_computation.7 | async-start | bytes 262144 | tf_op jit(solution)/shard_map/all_to_all | solution.py:158
  271.7 8.1 %all-to-all-start.10 = ((f32[32,4,256]{2,0,1:T(8,128)}), f32[32,4,256]{2,0,1:T(8,128)S(1)}, u32[]{:S(2)}, u32[]{:S(2)}) async-start(f32[32,4,256]{2,0,1:T(8,128)} %fusion), calls=%async_computation.11 | async-start | bytes 262144 | tf_op jit(solution)/shard_map/all_to_all | solution.py:159
  279.8 10.4 %all-to-all-start.7 = ((f32[4,128,256]{2,1,0:T(8,128)}), f32[4,128,256]{2,1,0:T(8,128)S(1)}, u32[]{:S(2)}, u32[]{:S(2)}) async-start(f32[4,128,256]{2,1,0:T(8,128)} %convolution_bitcast_fusion.1), calls=%async_computation.8 | async-start | bytes 1048576 | tf_op jit(solution)/shard_map/all_to_all | solution.py:65
  290.2 43.4 %all-to-all-start.8 = ((f32[64,16,256]{2,1,0:T(8,128)}), f32[64,16,256]{2,1,0:T(8,128)S(1)}, u32[]{:S(2)}, u32[]{:S(2)}) async-start(f32[64,16,256]{2,1,0:T(8,128)} %bitcast.25), calls=%async_computation.9 | async-start | bytes 2097152 | tf_op jit(solution)/shard_map/all_to_all | solution.py:65
Sparse Core Ops, SparseCore 0:
  180.0 80.6 reduce-scatter.1
